TPU v7x, 32 devices: a whole 2x2x4 slice. The times are simulated.
32 devices in a mesh: draws: 2 (over x), rows: 16 (over z, y, core).
Axes of the slice: x: 2, y: 2, z: 4, core: 2. Of those that a mesh axis runs over, the one named last changes fastest.
Arguments:
- leaf_rhs: bfloat16 [192, 256, 256], P('rows'), may hold values from -6 to 6
- separator_rhs: bfloat16 [4, 16, 256, 256], P(None, 'rows'), may hold values from -6 to 6
- leaf_inverse: bfloat16 [384, 256, 256], P(('draws', 'rows')), parts along dimension 0, as said below
- leaf_factor: bfloat16 [256, 4, 256, 256], P(('draws', 'rows')), parts along dimension 0, may hold values from -0.125 to 0.125
- separator_inverse: bfloat16 [4, 32, 256, 256], P(None, ('draws', 'rows')), parts along dimension 1, as said below
- separator_factor: bfloat16 [4, 32, 2, 256, 256], P(None, ('draws', 'rows')), parts along dimension 1, may hold values from -0.1875 to 0.1875
- block_pattern: int32 [128, 4], P('rows'), may hold values from 0 to 7, as said below
- link_row: int32 [16], P('rows'), may hold values from 8 to 11
Outputs:
- leaf_solution: bfloat16 [384, 256, 256], P(('draws', 'rows')), parts along dimension 0
- separator_solution: bfloat16 [4, 32, 256, 256], P(None, ('draws', 'rows')), parts along dimension 1
There are 2 independent parts, one for each index of `draws`. A program takes and returns all parts, laid end to end along the dimension named above; an argument that names none is the same for every part. Nothing has to cross between parts.
Inputs may be any that keep to these rules, and one draw needn't show every extreme that they name: `block_pattern`: for a block row on leaf level v >= 1 the 4 entries are distinct and below v * 4. `leaf_inverse`: every block is invertible. `separator_inverse`: every block is invertible.
All inputs are finite; a program needn't handle non-finite values.
Results may differ from a plain program's by a relative error of at most 0.011.
Values may be sent and summed in bfloat16 or wider, within the bound.
A program may use at most 64 MiB of HBM per device.

v0:
```python
import jax
import jax.numpy as jnp
from jax import lax
from jax.sharding import PartitionSpec as P

LEVEL_ROWS = 4
LEAF_LEVELS = 3


def passed_along(value, axis, by):
    length = lax.axis_size(axis)
    return lax.ppermute(value, axis, [(i, (i + by) % length) for i in range(length)])


def leaf_solve(rhs_piece, leaf_inverse, leaf_factor, block_pattern):
    solved = jnp.einsum(
        "nij,njr->nir",
        leaf_inverse[:LEVEL_ROWS],
        rhs_piece[:LEVEL_ROWS],
        preferred_element_type=jnp.float32,
    ).astype(jnp.bfloat16)
    for height in range(1, LEAF_LEVELS):
        low_row = (height - 1) * LEVEL_ROWS
        top_row = height * LEVEL_ROWS
        picked = jnp.take(solved, block_pattern[low_row:top_row], axis=0)
        accumulated = jnp.einsum(
            "nkij,nkjr->nir",
            leaf_factor[low_row:top_row],
            picked,
            preferred_element_type=jnp.float32,
        )
        residual = (
            rhs_piece[top_row : top_row + LEVEL_ROWS].astype(jnp.float32) - accumulated
        ).astype(jnp.bfloat16)
        fresh_rows = jnp.einsum(
            "nij,njr->nir",
            leaf_inverse[top_row : top_row + LEVEL_ROWS],
            residual,
            preferred_element_type=jnp.float32,
        ).astype(jnp.bfloat16)
        solved = jnp.concatenate([solved, fresh_rows], axis=0)
    return solved


def node_solve(lower_in, upper_in, rhs_node, inverse_node, factor_node):
    accumulated = jnp.dot(factor_node[0], lower_in, preferred_element_type=jnp.float32)
    accumulated = accumulated + jnp.dot(
        factor_node[1], upper_in, preferred_element_type=jnp.float32
    )
    residual = (rhs_node.astype(jnp.float32) - accumulated).astype(jnp.bfloat16)
    return jnp.dot(inverse_node, residual, preferred_element_type=jnp.float32).astype(jnp.bfloat16)


def level_solve(solved, link_row, separator_rhs, separator_inverse, separator_factor):
    depth = separator_rhs.shape[0]
    edge_block = lax.dynamic_index_in_dim(solved, link_row[0], 0, keepdims=False)
    from_lower = passed_along(edge_block, "rows", 1)
    level_block = node_solve(
        from_lower, edge_block, separator_rhs[0, 0], separator_inverse[0, 0], separator_factor[0, 0]
    )
    levels = [level_block]
    for height in range(1, depth):
        stride = 2 ** (height - 1)
        lower_child = passed_along(level_block, "rows", stride)
        upper_child = passed_along(level_block, "rows", -stride)
        level_block = node_solve(
            lower_child,
            upper_child,
            separator_rhs[height, 0],
            separator_inverse[height, 0],
            separator_factor[height, 0],
        )
        levels.append(level_block)
    return jnp.stack(levels, axis=0)[:, None]


def shards(
    leaf_rhs,
    separator_rhs,
    leaf_inverse,
    leaf_factor,
    separator_inverse,
    separator_factor,
    block_pattern,
    link_row,
):
    solved = leaf_solve(leaf_rhs, leaf_inverse, leaf_factor, block_pattern)
    return (
        solved,
        level_solve(solved, link_row, separator_rhs, separator_inverse, separator_factor),
    )


def solution(mesh):
    placed = (
        P("rows", None, None),
        P(None, "rows", None, None),
        P(("draws", "rows"), None, None),
        P(("draws", "rows"), None, None, None),
        P(None, ("draws", "rows"), None, None),
        P(None, ("draws", "rows"), None, None, None),
        P("rows", None),
        P("rows"),
    )
    return jax.shard_map(
        shards,
        mesh=mesh,
        in_specs=placed,
        out_specs=(P(("draws", "rows"), None, None), P(None, ("draws", "rows"), None, None)),
        check_vma=False,
    )
```

profile of v0, /device:TPU:0, one launch (start us, length us, event | category | flops | bytes accessed | tf_op | source)
XLA Modules:
  0.0 58.9 jit_solution(13481023518071097909)
XLA Ops:
  0.6 0.8 %compare_select_fusion = (s32[4,4]{0,1:T(4,128)S(1)}, s32[4,4]{0,1:T(4,128)S(1)}) fusion(s32[8,4]{0,1:T(4,128)} %param.14), kind=kLoop, calls=%fused_computation.95 | loop fusion | flops 96 | bytes 256 | tf_op jit(solution)/shard_map/jit(_take)/jit(_where)/select_n | solution.py:25
  1.5 0.8 %compare_and_fusion = (pred[4,4]{0,1:T(4,128)(4,1)S(1)}, pred[4,4]{0,1:T(4,128)(4,1)S(1)}) fusion(s32[8,4]{0,1:T(4,128)} %param.14), kind=kLoop, calls=%fused_computation.99 | loop fusion | flops 192 | bytes 160 | tf_op jit(solution)/shard_map/jit(_take)/and | solution.py:25
  2.3 0.1 copy.11
  2.4 0.1 reshape.44
  2.5 0.1 copy.10
  2.6 1.5 %convolution_convert_fusion.2 = bf16[4,256,256]{2,1,0:T(8,128)(2,1)S(1)} fusion(bf16[12,256,256]{2,1,0:T(8,128)(2,1)} %param.10, bf16[12,256,256]{2,1,0:T(8,128)(2,1)} %param.8), kind=kOutput, calls=%fused_computation.19 | convolution fusion | flops 134479872 | bytes 2621440 | tf_op jit(solution)/shard_map/nij,njr->nir/dot_general | solution.py:16
  4.1 0.7 %gather_fusion = bf16[16,256,256]{2,1,0:T(8,128)(2,1)S(1)} fusion(bf16[4,256,256]{2,1,0:T(8,128)(2,1)S(1)} %convolution_convert_fusion.2, s32[1024]{0:T(1024)S(1)} %pad_clamp_fusion.1), kind=kCustom, calls=%fused_computation | custom fusion | bytes 4194368 | tf_op jit(solution)/shard_map/jit(_take)/gather | solution.py:25
  4.8 2.9 %fusion.38 = bf16[4,256,256]{2,1,0:T(8,128)(2,1)S(1)} fusion(bf16[4,4,256,256]{3,2,1,0:T(8,128)(2,1)S(1)} %bitcast.157, pred[4,4]{1,0:T(4,128)(4,1)S(1)} %copy.10, bf16[8,4,256,256]{3,2,1,0:T(8,128)(2,1)} %param.11, bf16[12,256,256]{2,1,0:T(8,128)(2,1)} %param.10, bf16[12,256,256]{2,1,0:T(8,128)(2,1)} %param.8), kind=kOutput, calls=%fused_computation.20 | convolution fusion | flops 673185792 | bytes 5767184 | tf_op jit(solution)/shard_map/nij,njr->nir/dot_general | solution.py:35
  7.7 0.1 pad_maximum_fusion.1
  7.8 0.1 copy.15
  7.9 0.1 reshape.52
  7.9 0.1 copy.14
  8.1 2.0 %gather_fusion.1 = bf16[16,256,256]{2,1,0:T(8,128)(2,1)} fusion(bf16[8,256,256]{2,1,0:T(8,128)(2,1)S(1)} %pad_maximum_fusion.1, s32[1024]{0:T(1024)S(1)} %pad_clamp_fusion), kind=kCustom, calls=%fused_computation.1 | custom fusion | bytes 4194368 | tf_op jit(solution)/shard_map/jit(_take)/gather | solution.py:25
  10.1 4.3 %fusion.39 = bf16[4,256,256]{2,1,0:T(8,128)(2,1)} fusion(bf16[4,4,256,256]{3,2,1,0:T(8,128)(2,1)} %bitcast.156, pred[4,4]{1,0:T(4,128)(4,1)S(1)} %copy.14, bf16[8,4,256,256]{3,2,1,0:T(8,128)(2,1)} %param.11, bf16[12,256,256]{2,1,0:T(8,128)(2,1)} %param.10, bf16[12,256,256]{2,1,0:T(8,128)(2,1)} %param.8), kind=kOutput, calls=%fused_computation.21 | convolution fusion | flops 673185792 | bytes 5767184 | tf_op jit(solution)/shard_map/nij,njr->nir/dot_general | solution.py:35
  14.3 0.0 copy-start.2
  14.3 1.3 %pad_maximum_fusion = bf16[12,256,256]{2,1,0:T(8,128)(2,1)S(1)} fusion(bf16[4,256,256]{2,1,0:T(8,128)(2,1)} %fusion.39, bf16[4,256,256]{2,1,0:T(8,128)(2,1)S(1)} %fusion.38, bf16[4,256,256]{2,1,0:T(8,128)(2,1)S(1)} %convolution_convert_fusion.2), kind=kLoop, calls=%fused_computation.10 | loop fusion | flops 1572864 | bytes 3145728 | tf_op jit(solution)/shard_map/concatenate | solution.py:41
  15.6 0.0 copy-start
  15.6 0.0 copy-start.1
  16.4 0.5 collective-permute-start
  16.9 1.1 %fusion.96 = f32[256,256]{0,1:T(8,128)S(1)} fusion(bf16[256,256]{1,0:T(8,128)(2,1)S(1)} %dynamic-slice_bitcast_fusion, bf16[4,1,2,256,256]{4,3,2,1,0:T(8,128)(2,1)} %param.13), kind=kOutput, calls=%fused_computation.75 | convolution fusion | flops 33554432 | bytes 524288 | tf_op jit(solution)/shard_map/dot_general | solution.py:47
  18.0 6.7 %collective-permute-done = bf16[256,256]{1,0:T(8,128)(2,1)} collective-permute-done((bf16[256,256]{1,0:T(8,128)(2,1)S(1)}, bf16[256,256]{1,0:T(8,128)(2,1)}, u32[]{:S(2)}, u32[]{:S(2)}) %collective-permute-start) | collective-permute-done | bytes 131104 | tf_op jit(solution)/shard_map/ppermute | solution.py:12
  24.7 0.0 copy-done.2
  24.7 1.5 %convolution_convert_fusion.6 = bf16[256,256]{1,0:T(8,128)(2,1)S(1)} fusion(f32[256,256]{0,1:T(8,128)S(1)} %fusion.96, bf16[256,256]{1,0:T(8,128)(2,1)} %collective-permute-done, bf16[4,1,256,256]{3,2,1,0:T(8,128)(2,1)S(1)} %copy-done.2, bf16[4,1,2,256,256]{4,3,2,1,0:T(8,128)(2,1)} %param.13, bf16[4,1,256,256]{3,2,1,0:T(8,128)(2,1)} %param.9), kind=kOutput, calls=%fused_computation.41 | convolution fusion | flops 67436544 | bytes 917504 | tf_op jit(solution)/shard_map/dot_general | solution.py:51
  26.2 0.1 collective-permute-start.2
  26.2 0.5 collective-permute-start.1
  26.7 2.0 %collective-permute-done.2 = bf16[256,256]{0,1:T(8,128)(2,1)S(1)} collective-permute-done((bf16[256,256]{0,1:T(8,128)(2,1)S(1)}, bf16[256,256]{0,1:T(8,128)(2,1)S(1)}, u32[]{:S(2)}, u32[]{:S(2)}) %collective-permute-start.2) | collective-permute-done | bytes 131104 | tf_op jit(solution)/shard_map/ppermute | solution.py:12
  28.7 1.1 %fusion.91 = f32[256,256]{0,1:T(8,128)S(1)} fusion(bf16[256,256]{0,1:T(8,128)(2,1)S(1)} %collective-permute-done.2, bf16[4,1,2,256,256]{4,3,2,1,0:T(8,128)(2,1)} %param.13), kind=kOutput, calls=%fused_computation.71 | convolution fusion | flops 33554432 | bytes 524288 | tf_op jit(solution)/shard_map/dot_general | solution.py:47
  29.9 3.6 %collective-permute-done.1 = bf16[256,256]{0,1:T(8,128)(2,1)} collective-permute-done((bf16[256,256]{0,1:T(8,128)(2,1)S(1)}, bf16[256,256]{0,1:T(8,128)(2,1)}, u32[]{:S(2)}, u32[]{:S(2)}) %collective-permute-start.1) | collective-permute-done | bytes 131104 | tf_op jit(solution)/shard_map/ppermute | solution.py:12
  33.5 0.0 copy-done.1
  33.5 2.1 %convolution_convert_fusion.5 = bf16[256,256]{1,0:T(8,128)(2,1)} fusion(f32[256,256]{0,1:T(8,128)S(1)} %fusion.91, bf16[256,256]{0,1:T(8,128)(2,1)} %collective-permute-done.1, bf16[4,1,256,256]{3,2,1,0:T(8,128)(2,1)S(1)} %copy-done.2, bf16[4,1,2,256,256]{4,3,2,1,0:T(8,128)(2,1)S(1)} %copy-done.1, bf16[4,1,256,256]{3,2,1,0:T(8,128)(2,1)} %param.9), kind=kOutput, calls=%fused_computation.40 | convolution fusion | flops 67436544 | bytes 917504 | tf_op jit(solution)/shard_map/dot_general | solution.py:51
  35.6 1.0 %collective-permute-start.4 = (bf16[256,256]{0,1:T(8,128)(2,1)}, bf16[256,256]{0,1:T(8,128)(2,1)S(1)}, u32[]{:S(2)}, u32[]{:S(2)}) collective-permute-start(bf16[256,256]{0,1:T(8,128)(2,1)} %bitcast.161), channel_id=1, source_target_pairs={{0,14},{1,15},{2,0},{3,1},{4,2},{5,3},{6,4},{7,5},{8,6},{9,7},{10,... | collective-permute-start | bytes 393224 | tf_op jit(solution)/shard_map/ppermute | solution.py:12
  36.6 1.0 %collective-permute-start.3 = (bf16[256,256]{0,1:T(8,128)(2,1)}, bf16[256,256]{0,1:T(8,128)(2,1)}, u32[]{:S(2)}, u32[]{:S(2)}) collective-permute-start(bf16[256,256]{0,1:T(8,128)(2,1)} %bitcast.162), channel_id=1, source_target_pairs={{0,2},{1,3},{2,4},{3,5},{4,6},{5,7},{6,8},{7,9},{8,10},{9,11},{10,... | collective-permute-start | bytes 393224 | tf_op jit(solution)/shard_map/ppermute | solution.py:12
  37.6 3.2 %collective-permute-done.4 = bf16[256,256]{0,1:T(8,128)(2,1)S(1)} collective-permute-done((bf16[256,256]{0,1:T(8,128)(2,1)}, bf16[256,256]{0,1:T(8,128)(2,1)S(1)}, u32[]{:S(2)}, u32[]{:S(2)}) %collective-permute-start.4) | collective-permute-done | bytes 131104 | tf_op jit(solution)/shard_map/ppermute | solution.py:12
  40.8 0.2 fusion.86
  41.0 4.2 %collective-permute-done.3 = bf16[256,256]{0,1:T(8,128)(2,1)} collective-permute-done((bf16[256,256]{0,1:T(8,128)(2,1)}, bf16[256,256]{0,1:T(8,128)(2,1)}, u32[]{:S(2)}, u32[]{:S(2)}) %collective-permute-start.3) | collective-permute-done | bytes 131104 | tf_op jit(solution)/shard_map/ppermute | solution.py:12
  45.2 2.1 %convolution_convert_fusion.4 = bf16[256,256]{1,0:T(8,128)(2,1)} fusion(f32[256,256]{0,1:T(8,128)S(1)} %fusion.86, bf16[256,256]{0,1:T(8,128)(2,1)} %collective-permute-done.3, bf16[4,1,256,256]{3,2,1,0:T(8,128)(2,1)S(1)} %copy-done.2, bf16[4,1,2,256,256]{4,3,2,1,0:T(8,128)(2,1)S(1)} %copy-done.1, bf16[4,1,256,256]{3,2,1,0:T(8,128)(2,1)} %param.9), kind=kOutput, calls=%fused_computation.39 | convolution fusion | flops 67436544 | bytes 917504 | tf_op jit(solution)/shard_map/dot_general | solution.py:51
  47.3 0.0 copy-done
  47.3 0.0 collective-permute-start.6
  47.3 2.0 %collective-permute-start.5 = (bf16[256,256]{0,1:T(8,128)(2,1)}, bf16[256,256]{0,1:T(8,128)(2,1)S(1)}, u32[]{:S(2)}, u32[]{:S(2)}) collective-permute-start(bf16[256,256]{0,1:T(8,128)(2,1)} %bitcast.165), channel_id=1, source_target_pairs={{0,4},{1,5},{2,6},{3,7},{4,8},{5,9},{6,10},{7,11},{8,12},{9,13},{1... | collective-permute-start | bytes 393224 | tf_op jit(solution)/shard_map/ppermute | solution.py:12
  49.3 6.0 %collective-permute-done.6 = bf16[256,256]{0,1:T(8,128)(2,1)S(1)} collective-permute-done((bf16[256,256]{0,1:T(8,128)(2,1)}, bf16[256,256]{0,1:T(8,128)(2,1)S(1)}, u32[]{:S(2)}, u32[]{:S(2)}) %collective-permute-start.6) | collective-permute-done | bytes 131104 | tf_op jit(solution)/shard_map/ppermute | solution.py:12
  55.3 0.2 fusion.81
  55.5 0.0 collective-permute-done.5
  55.5 1.4 %fusion.60 = bf16[1,256,256]{1,2,0:T(8,128)(2,1)S(1)} fusion(f32[256,256]{0,1:T(8,128)S(1)} %fusion.81, bf16[256,256]{0,1:T(8,128)(2,1)S(1)} %collective-permute-done.5, bf16[4,1,256,256]{3,2,1,0:T(8,128)(2,1)S(1)} %copy-done.2, bf16[4,1,2,256,256]{4,3,2,1,0:T(8,128)(2,1)S(1)} %copy-done.1, bf16[4,1,256,256]{3,2,1,0:T(8,128)(2,1)} %param.9), kind=kOutput, calls=%fused_computation.42 | convolution fusion | flops 67436544 | bytes 917504 | tf_op jit(solution)/shard_map/dot_general | solution.py:51
  56.9 1.0 %maximum_bitcast_fusion = bf16[4,1,256,256]{2,3,0,1:T(8,128)(2,1)S(1)} fusion(bf16[1,256,256]{1,2,0:T(8,128)(2,1)S(1)} %fusion.60, bf16[1,256,256]{1,2,0:T(8,128)(2,1)} %bitcast.166, bf16[1,256,256]{1,2,0:T(8,128)(2,1)} %bitcast.163, bf16[1,256,256]{1,2,0:T(8,128)(2,1)S(1)} %bitcast.160), kind=kLoop, calls=%fused_computation.48 | loop fusion | flops 786432 | bytes 1048576 | tf_op jit(solution)/shard_map/broadcast_in_dim | solution.py:74
  57.9 1.0 %copy.18 = bf16[4,1,256,256]{3,2,1,0:T(8,128)(2,1)} copy(bf16[4,1,256,256]{2,3,0,1:T(8,128)(2,1)S(1)} %maximum_bitcast_fusion) | data formatting | bytes 1048576
  (3 shorter events, 0.0 us)
Async XLA Ops:
  14.3 10.3 %copy-start.2 = (bf16[4,1,256,256]{3,2,1,0:T(8,128)(2,1)S(1)}, bf16[4,1,256,256]{3,2,1,0:T(8,128)(2,1)}, u32[]{:S(2)}) copy-start(bf16[4,1,256,256]{3,2,1,0:T(8,128)(2,1)} %param.12) | copy-start | bytes 1572868
  15.6 31.7 %copy-start = (bf16[12,256,256]{2,1,0:T(8,128)(2,1)}, bf16[12,256,256]{2,1,0:T(8,128)(2,1)S(1)}, u32[]{:S(2)}) copy-start(bf16[12,256,256]{2,1,0:T(8,128)(2,1)S(1)} %pad_maximum_fusion) | copy-start | bytes 4718596
  15.6 17.8 %copy-start.1 = (bf16[4,1,2,256,256]{4,3,2,1,0:T(8,128)(2,1)S(1)}, bf16[4,1,2,256,256]{4,3,2,1,0:T(8,128)(2,1)}, u32[]{:S(2)}) copy-start(bf16[4,1,2,256,256]{4,3,2,1,0:T(8,128)(2,1)} %param.13) | copy-start | bytes 3145732
  16.4 8.3 %collective-permute-start = (bf16[256,256]{1,0:T(8,128)(2,1)S(1)}, bf16[256,256]{1,0:T(8,128)(2,1)}, u32[]{:S(2)}, u32[]{:S(2)}) collective-permute-start(bf16[256,256]{1,0:T(8,128)(2,1)S(1)} %dynamic-slice_bitcast_fusion), channel_id=1, source_target_pairs={{0,1},{1,2},{2,3},{3,4},{4,5},{5,6},{6,7},{7,8},{8,9},{9,10},{10,1... | collective-permute-start | bytes 393224 | tf_op jit(solution)/shard_map/ppermute | solution.py:12
  26.2 2.6 %collective-permute-start.2 = (bf16[256,256]{0,1:T(8,128)(2,1)S(1)}, bf16[256,256]{0,1:T(8,128)(2,1)S(1)}, u32[]{:S(2)}, u32[]{:S(2)}) collective-permute-start(bf16[256,256]{0,1:T(8,128)(2,1)S(1)} %bitcast.158), channel_id=1, source_target_pairs={{0,15},{1,0},{2,1},{3,2},{4,3},{5,4},{6,5},{7,6},{8,7},{9,8},{10,9... | collective-permute-start | bytes 393224 | tf_op jit(solution)/shard_map/ppermute | solution.py:12
  26.2 7.2 %collective-permute-start.1 = (bf16[256,256]{0,1:T(8,128)(2,1)S(1)}, bf16[256,256]{0,1:T(8,128)(2,1)}, u32[]{:S(2)}, u32[]{:S(2)}) collective-permute-start(bf16[256,256]{0,1:T(8,128)(2,1)S(1)} %bitcast.159), channel_id=1, source_target_pairs={{0,1},{1,2},{2,3},{3,4},{4,5},{5,6},{6,7},{7,8},{8,9},{9,10},{10,1... | collective-permute-start | bytes 393224 | tf_op jit(solution)/shard_map/ppermute | solution.py:12
  35.6 5.2 %collective-permute-start.4 = (bf16[256,256]{0,1:T(8,128)(2,1)}, bf16[256,256]{0,1:T(8,128)(2,1)S(1)}, u32[]{:S(2)}, u32[]{:S(2)}) collective-permute-start(bf16[256,256]{0,1:T(8,128)(2,1)} %bitcast.161), channel_id=1, source_target_pairs={{0,14},{1,15},{2,0},{3,1},{4,2},{5,3},{6,4},{7,5},{8,6},{9,7},{10,... | collective-permute-start | bytes 393224 | tf_op jit(solution)/shard_map/ppermute | solution.py:12
  36.6 8.6 %collective-permute-start.3 = (bf16[256,256]{0,1:T(8,128)(2,1)}, bf16[256,256]{0,1:T(8,128)(2,1)}, u32[]{:S(2)}, u32[]{:S(2)}) collective-permute-start(bf16[256,256]{0,1:T(8,128)(2,1)} %bitcast.162), channel_id=1, source_target_pairs={{0,2},{1,3},{2,4},{3,5},{4,6},{5,7},{6,8},{7,9},{8,10},{9,11},{10,... | collective-permute-start | bytes 393224 | tf_op jit(solution)/shard_map/ppermute | solution.py:12
  47.3 8.0 %collective-permute-start.6 = (bf16[256,256]{0,1:T(8,128)(2,1)}, bf16[256,256]{0,1:T(8,128)(2,1)S(1)}, u32[]{:S(2)}, u32[]{:S(2)}) collective-permute-start(bf16[256,256]{0,1:T(8,128)(2,1)} %bitcast.164), channel_id=1, source_target_pairs={{0,12},{1,13},{2,14},{3,15},{4,0},{5,1},{6,2},{7,3},{8,4},{9,5},{1... | collective-permute-start | bytes 393224 | tf_op jit(solution)/shard_map/ppermute | solution.py:12
  47.3 8.2 %collective-permute-start.5 = (bf16[256,256]{0,1:T(8,128)(2,1)}, bf16[256,256]{0,1:T(8,128)(2,1)S(1)}, u32[]{:S(2)}, u32[]{:S(2)}) collective-permute-start(bf16[256,256]{0,1:T(8,128)(2,1)} %bitcast.165), channel_id=1, source_target_pairs={{0,4},{1,5},{2,6},{3,7},{4,8},{5,9},{6,10},{7,11},{8,12},{9,13},{1... | collective-permute-start | bytes 393224 | tf_op jit(solution)/shard_map/ppermute | solution.py:12
where the time goes:
time: 59.3 us; the launch traced here: 58.9 us
  waiting for transfers between devices  25.6 us (43%)
  matrix products  18.3 us (31%)
  starting transfers between devices  5.11 us (9%)
  local copies, waits for them, and re-layouts  4.29 us (7%)
  other arithmetic  4.08 us (7%)
  between operations  1.54 us (3%)
    ppermute x7, waiting for transfers between devices, passed_along(): lax.ppermute(value, axis, [(i, (i + by) % length) for i in range(length)])  25.6 us
    dot_general x2, matrix products, leaf_solve(): jnp.einsum('nij,njr->nir', leaf_inverse[top_row:top_row + LEVEL_ROWS], re...  7.14 us
    dot_general x4, matrix products, node_solve(): jnp.dot(inverse_node, residual, preferred_element_type=jnp.float32)  7.03 us
    ppermute x7, starting transfers between devices, passed_along(): lax.ppermute(value, axis, [(i, (i + by) % length) for i in range(length)])  5.11 us
    gather x2, local copies, waits for them, and re-layouts, leaf_solve(): picked = jnp.take(solved, block_pattern[low_row:top_row], axis=0)  2.69 us
    dot_general x4, matrix products, node_solve(): jnp.dot(factor_node[1], upper_in, preferred_element_type=jnp.float32)  2.63 us
    dot_general x1, matrix products, leaf_solve(): jnp.einsum('nij,njr->nir', leaf_inverse[:LEVEL_ROWS], rhs_piece[:LEVEL_RO...  1.5 us
    concatenate x2, other arithmetic, leaf_solve(): solved = jnp.concatenate([solved, fresh_rows], axis=0)  1.36 us
  transfers between devices with their start and end apart: 7, of which 6 were waited for; matrix products, arithmetic and copies ran while one was open for 4% of the time, Pallas kernels for 0%

commit v1 on v0

v1 whole, which is shorter than its diff:
```python
import functools

import jax
import jax.numpy as jnp
from jax import lax
from jax.experimental import pallas as pl
from jax.experimental.pallas import tpu as pltpu
from jax.sharding import PartitionSpec as P

LEVEL_ROWS = 4
LEAF_LEVELS = 3
CHUNKS = 2
F32 = jnp.float32
BF16 = jnp.bfloat16


def dot(a, b):
    return jnp.dot(a, b, preferred_element_type=F32)


def kernel(
    n,
    depth,
    relay_level,
    rhs_hbm,
    sep_rhs_hbm,
    inv_hbm,
    fac_hbm,
    sep_inv_hbm,
    sep_fac_hbm,
    pattern,
    link,
    leaf_out,
    sep_out,
    rhs,
    inv,
    fac,
    sep_rhs,
    sep_inv,
    sep_fac,
    solved,
    edge,
    sol,
    recv,
    load_sem,
    leaf_sem,
    out_sem,
    send_sem,
    recv_sem,
):
    me = lax.axis_index("rows")
    coupled = fac.shape[1]
    width = sol.shape[-1]

    def peer(by):
        return lax.rem(me + (by % n), n)

    loads = {}

    def load(name, src, dst):
        copy = pltpu.make_async_copy(src, dst, load_sem.at[len(loads)])
        copy.start()
        loads[name] = copy

    for level in range(LEAF_LEVELS):
        rows = pl.ds(level * LEVEL_ROWS, LEVEL_ROWS)
        if level:
            low = pl.ds((level - 1) * LEVEL_ROWS, LEVEL_ROWS)
            load(("fac", level), fac_hbm.at[low], fac.at[low])
        load(("rhs", level), rhs_hbm.at[rows], rhs.at[rows])
        load(("inv", level), inv_hbm.at[rows], inv.at[rows])
    load("sep_fac", sep_fac_hbm.at[:, 0], sep_fac)
    load("sep_rhs", sep_rhs_hbm.at[:, 0], sep_rhs)
    load("sep_inv", sep_inv_hbm.at[:, 0], sep_inv)

    offsets = sorted({(sign * 2**h) % n for h in range(depth - 1) for sign in (1, -1)})
    barrier = pltpu.get_barrier_semaphore()
    for by in offsets:
        pl.semaphore_signal(
            barrier, inc=1, device_id={"rows": peer(by)}, device_id_type=pl.DeviceIdType.MESH
        )

    def residual(row, q):
        total = dot(fac[q, 0], solved[pattern[q, 0]])
        for k in range(1, coupled):
            total += dot(fac[q, k], solved[pattern[q, k]])
        return (rhs[row].astype(F32) - total).astype(BF16)

    out_copies = []

    def leaf_write(level):
        rows = pl.ds(level * LEVEL_ROWS, LEVEL_ROWS)
        copy = pltpu.make_async_copy(solved.at[rows], leaf_out.at[rows], leaf_sem.at[level])
        copy.start()
        out_copies.append(copy)

    loads[("rhs", 0)].wait()
    loads[("inv", 0)].wait()
    for row in range(LEVEL_ROWS):
        solved[row] = dot(inv[row], rhs[row]).astype(BF16)
    leaf_write(0)

    def leaf_level(level):
        first = level * LEVEL_ROWS
        parts = [residual(first + i, first - LEVEL_ROWS + i) for i in range(LEVEL_ROWS)]
        for i in range(LEVEL_ROWS):
            solved[first + i] = dot(inv[first + i], parts[i]).astype(BF16)
        leaf_write(level)

    for level in range(1, LEAF_LEVELS - 1):
        for name in ("fac", "rhs", "inv"):
            loads[(name, level)].wait()
        leaf_level(level)

    top = LEAF_LEVELS - 1
    for name in ("fac", "rhs", "inv"):
        loads[(name, top)].wait()
    link_row = link[0]
    edge_block = dot(inv[link_row], residual(link_row, jnp.maximum(link_row - LEVEL_ROWS, 0))).astype(BF16)
    for j in range(CHUNKS):
        edge[j] = edge_block[:, j * width : (j + 1) * width]

    pl.semaphore_wait(barrier, len(offsets))

    sends = []

    def send(src, level, side, j, to, slot):
        copy = pltpu.make_async_remote_copy(
            src_ref=src,
            dst_ref=recv.at[level, side, j],
            send_sem=send_sem.at[level, slot, j],
            recv_sem=recv_sem.at[level, side, j],
            device_id={"rows": to},
            device_id_type=pl.DeviceIdType.MESH,
        )
        copy.start()
        sends.append(copy)

    def arrived(level, side, j):
        pltpu.make_async_remote_copy(
            src_ref=edge.at[j],
            dst_ref=recv.at[level, side, j],
            send_sem=send_sem.at[level, 0, j],
            recv_sem=recv_sem.at[level, side, j],
            device_id={"rows": peer(1)},
            device_id_type=pl.DeviceIdType.MESH,
        ).wait_recv()

    for j in range(CHUNKS):
        send(edge.at[j], 0, 0, j, peer(1), 0)

    leaf_level(top)

    loads["sep_fac"].wait()
    loads["sep_rhs"].wait()
    loads["sep_inv"].wait()

    y = lax.rem(lax.div(me, 2), 2)
    for level in range(depth):
        for j in range(CHUNKS):
            columns = slice(j * width, (j + 1) * width)
            if level == 0:
                total = dot(sep_fac[level, 1], edge[j])
                arrived(level, 0, j)
                total += dot(sep_fac[level, 0], recv[level, 0, j])
            elif level == relay_level:
                stride = 2 ** (level - 1)
                near, far = 1 - y, y
                arrived(level, near, j)
                beyond = lax.rem(me + 2 * stride + (n - 4 * stride) * y, n)
                send(recv.at[level, near, j], level, far, j, beyond, 1)
                total = dot(sep_fac[level, near], recv[level, near, j])
                arrived(level, far, j)
                total += dot(sep_fac[level, far], recv[level, far, j])
            else:
                arrived(level, 0, j)
                total = dot(sep_fac[level, 0], recv[level, 0, j])
                arrived(level, 1, j)
                total += dot(sep_fac[level, 1], recv[level, 1, j])
            part = (sep_rhs[level, :, columns].astype(F32) - total).astype(BF16)
            sol[level, j] = dot(sep_inv[level], part).astype(BF16)
            if level + 1 < depth:
                stride = 2**level
                if level + 1 == relay_level:
                    across = lax.rem(me + stride + (n - 2 * stride) * y, n)
                    send(sol.at[level, j], level + 1, y, j, across, 0)
                else:
                    send(sol.at[level, j], level + 1, 0, j, peer(stride), 0)
                    send(sol.at[level, j], level + 1, 1, j, peer(-stride), 1)
            copy = pltpu.make_async_copy(
                sol.at[level, j], sep_out.at[level, 0, :, pl.ds(j * width, width)], out_sem.at[level, j]
            )
            copy.start()
            out_copies.append(copy)

    for copy in sends:
        copy.wait_send()
    for copy in out_copies:
        copy.wait()


def shards(n, leaf_rhs, separator_rhs, leaf_inverse, leaf_factor, separator_inverse, separator_factor, block_pattern, link_row):
    depth = separator_rhs.shape[0]
    block, loads = leaf_rhs.shape[1:]
    width = loads // CHUNKS
    upper, coupled = leaf_factor.shape[:2]
    matmuls = leaf_rhs.shape[0] + upper * coupled + 3 * depth
    hbm = pl.BlockSpec(memory_space=pl.ANY)
    smem = pl.BlockSpec(memory_space=pltpu.SMEM)
    return pl.pallas_call(
        functools.partial(kernel, n, depth, 2 if n == 16 else -1),
        out_shape=(
            jax.ShapeDtypeStruct(leaf_rhs.shape, BF16),
            jax.ShapeDtypeStruct(separator_rhs.shape, BF16),
        ),
        in_specs=[hbm] * 6 + [smem] * 2,
        out_specs=(hbm, hbm),
        scratch_shapes=[
            pltpu.VMEM(leaf_rhs.shape, BF16),
            pltpu.VMEM(leaf_inverse.shape, BF16),
            pltpu.VMEM(leaf_factor.shape, BF16),
            pltpu.VMEM((depth, block, loads), BF16),
            pltpu.VMEM((depth, block, block), BF16),
            pltpu.VMEM((depth, 2, block, block), BF16),
            pltpu.VMEM(leaf_rhs.shape, BF16),
            pltpu.VMEM((CHUNKS, block, width), BF16),
            pltpu.VMEM((depth, CHUNKS, block, width), BF16),
            pltpu.VMEM((depth, 2, CHUNKS, block, width), BF16),
            pltpu.SemaphoreType.DMA((3 * LEAF_LEVELS + 2,)),
            pltpu.SemaphoreType.DMA((LEAF_LEVELS,)),
            pltpu.SemaphoreType.DMA((depth, CHUNKS)),
            pltpu.SemaphoreType.DMA((depth, 2, CHUNKS)),
            pltpu.SemaphoreType.DMA((depth, 2, CHUNKS)),
        ],
        compiler_params=pltpu.CompilerParams(
            collective_id=0, has_side_effects=True, vmem_limit_bytes=48 * 2**20
        ),
        cost_estimate=pl.CostEstimate(
            flops=2 * matmuls * block * block * loads,
            bytes_accessed=2 * (matmuls + 2 * leaf_rhs.shape[0]) * block * loads,
            transcendentals=0,
        ),
        name="tree_solve",
    )(leaf_rhs, separator_rhs, leaf_inverse, leaf_factor, separator_inverse, separator_factor, block_pattern, link_row)


def solution(mesh):
    placed = (
        P("rows", None, None),
        P(None, "rows", None, None),
        P(("draws", "rows"), None, None),
        P(("draws", "rows"), None, None, None),
        P(None, ("draws", "rows"), None, None),
        P(None, ("draws", "rows"), None, None, None),
        P("rows", None),
        P("rows"),
    )
    return jax.shard_map(
        functools.partial(shards, mesh.shape["rows"]),
        mesh=mesh,
        in_specs=placed,
        out_specs=(P(("draws", "rows"), None, None), P(None, ("draws", "rows"), None, None)),
        check_vma=False,
    )
```

time: 59.3 us -> 39.6 us (0.67)
  the two profiles are of different devices: /device:TPU:0 before, /device:TPU:1 now
where the time goes in v1:
time: 39.6 us; the launch traced here: 39.3 us
  Pallas kernels  30.6 us (77%)
  local copies, waits for them, and re-layouts  7.41 us (19%)
  between operations  1.29 us (3%)
    pallas_call x1, Pallas kernels, shards(): pl.pallas_call(functools.partial(kernel, n, depth, 2 if n == 16 else -1),...  30.6 us
    unnamed x11, local copies, waits for them, and re-layouts  7.41 us

profile of v1, /device:TPU:1, one launch (start us, length us, event | category | flops | bytes accessed | tf_op | source)
XLA Modules:
  0.0 39.3 jit_solution(169199962223535241)
XLA Ops:
  1.3 0.8 %copy.10.pattern = s32[8,4]{1,0:T(8,128)S(1)} copy(s32[8,4]{0,1:T(4,128)} %param.14) | data formatting | bytes 256 | tf_op args[6]
  2.0 0.0 copy-start
  2.0 1.4 %copy-done = bf16[12,256,256]{2,1,0:T(8,128)(2,1)S(1)} copy-done((bf16[12,256,256]{2,1,0:T(8,128)(2,1)S(1)}, bf16[12,256,256]{2,1,0:T(8,128)(2,1)}, u32[]{:S(2)}) %copy-start) | copy-done | bytes 1572888
  3.4 0.0 copy-start.1
  3.4 1.2 %copy-done.1 = bf16[4,1,2,256,256]{4,3,2,1,0:T(8,128)(2,1)S(1)} copy-done((bf16[4,1,2,256,256]{4,3,2,1,0:T(8,128)(2,1)S(1)}, bf16[4,1,2,256,256]{4,3,2,1,0:T(8,128)(2,1)}, u32[]{:S(2)}) %copy-start.1) | copy-done | bytes 1048600
  4.7 0.0 copy-start.2
  4.7 1.0 %copy-done.2 = bf16[4,1,256,256]{3,2,1,0:T(8,128)(2,1)S(1)} copy-done((bf16[4,1,256,256]{3,2,1,0:T(8,128)(2,1)S(1)}, bf16[4,1,256,256]{3,2,1,0:T(8,128)(2,1)}, u32[]{:S(2)}) %copy-start.2) | copy-done | bytes 524312
  5.7 0.0 copy-start.3
  5.7 1.0 %copy-done.3 = bf16[4,1,256,256]{3,2,1,0:T(8,128)(2,1)S(1)} copy-done((bf16[4,1,256,256]{3,2,1,0:T(8,128)(2,1)S(1)}, bf16[4,1,256,256]{3,2,1,0:T(8,128)(2,1)}, u32[]{:S(2)}) %copy-start.3) | copy-done | bytes 524312
  6.8 30.6 %tree_solve.1 = (bf16[12,256,256]{2,1,0:T(8,128)(2,1)S(1)}, bf16[4,1,256,256]{3,2,1,0:T(8,128)(2,1)S(1)}) custom-call(bf16[12,256,256]{2,1,0:T(8,128)(2,1)S(1)} %copy-done, bf16[4,1,256,256]{3,2,1,0:T(8,128)(2,1)S(1)} %copy-done.2, bf16[12,256,256]{2,1,0:T(8,128)(2,1)} %inv_hbm.1, bf16[8,4,256,256]{3,2,1,0:T(8,128)(2,1)} %fac_hbm.1, ...), custom_call_target="tpu_custom_call" | custom-call | flops 1879048192 | bytes 10485760 | tf_op jit(solution)/shard_map/tree_solve/pallas_call | solution.py:210
  37.4 1.1 %copy.14 = bf16[12,256,256]{2,1,0:T(8,128)(2,1)} copy(bf16[12,256,256]{2,1,0:T(8,128)(2,1)S(1)} %get-tuple-element.4) | data formatting | bytes 3145728
  38.5 0.8 %copy.15 = bf16[4,1,256,256]{3,2,1,0:T(8,128)(2,1)} copy(bf16[4,1,256,256]{3,2,1,0:T(8,128)(2,1)S(1)} %get-tuple-element.5) | data formatting | bytes 1048576
Async XLA Ops:
  2.0 1.4 %copy-start = (bf16[12,256,256]{2,1,0:T(8,128)(2,1)S(1)}, bf16[12,256,256]{2,1,0:T(8,128)(2,1)}, u32[]{:S(2)}) copy-start(bf16[12,256,256]{2,1,0:T(8,128)(2,1)} %rhs_hbm.1) | copy-start | bytes 4718596
  3.4 1.2 %copy-start.1 = (bf16[4,1,2,256,256]{4,3,2,1,0:T(8,128)(2,1)S(1)}, bf16[4,1,2,256,256]{4,3,2,1,0:T(8,128)(2,1)}, u32[]{:S(2)}) copy-start(bf16[4,1,2,256,256]{4,3,2,1,0:T(8,128)(2,1)} %sep_fac_hbm.1) | copy-start | bytes 3145732
  4.7 1.0 %copy-start.2 = (bf16[4,1,256,256]{3,2,1,0:T(8,128)(2,1)S(1)}, bf16[4,1,256,256]{3,2,1,0:T(8,128)(2,1)}, u32[]{:S(2)}) copy-start(bf16[4,1,256,256]{3,2,1,0:T(8,128)(2,1)} %sep_rhs_hbm.1) | copy-start | bytes 1572868
  5.7 1.0 %copy-start.3 = (bf16[4,1,256,256]{3,2,1,0:T(8,128)(2,1)S(1)}, bf16[4,1,256,256]{3,2,1,0:T(8,128)(2,1)}, u32[]{:S(2)}) copy-start(bf16[4,1,256,256]{3,2,1,0:T(8,128)(2,1)} %sep_inv_hbm.1) | copy-start | bytes 1572868

commit v2 on v1

--- a/solution.py
+++ b/solution.py
@@ -40,6 +40,8 @@
     sep_fac,
     solved,
     edge,
+    weight,
+    free,
     sol,
     recv,
     load_sem,
@@ -81,9 +83,9 @@
         )
 
     def residual(row, q):
-        total = dot(fac[q, 0], solved[pattern[q, 0]])
+        total = dot(fac[q, 0], solved[pattern[0, q]])
         for k in range(1, coupled):
-            total += dot(fac[q, k], solved[pattern[q, k]])
+            total += dot(fac[q, k], solved[pattern[k, q]])
         return (rhs[row].astype(F32) - total).astype(BF16)
 
     out_copies = []
@@ -149,49 +151,54 @@
     for j in range(CHUNKS):
         send(edge.at[j], 0, 0, j, peer(1), 0)
 
-    leaf_level(top)
+    def prepare(level):
+        node_inv = sep_inv[level]
+        for side in range(2):
+            weight[level, side] = dot(node_inv, sep_fac[level, side]).astype(BF16)
+        free[level] = dot(node_inv, sep_rhs[level])
 
     loads["sep_fac"].wait()
     loads["sep_rhs"].wait()
     loads["sep_inv"].wait()
-
-    y = lax.rem(lax.div(me, 2), 2)
+    prepare(0)
+
     for level in range(depth):
+        stride = 2 ** max(level - 1, 0)
+        p = lax.rem(lax.div(me, stride), 2)
+        near, far = 1 - p, p
         for j in range(CHUNKS):
             columns = slice(j * width, (j + 1) * width)
             if level == 0:
-                total = dot(sep_fac[level, 1], edge[j])
+                total = dot(weight[level, 1], edge[j])
                 arrived(level, 0, j)
-                total += dot(sep_fac[level, 0], recv[level, 0, j])
-            elif level == relay_level:
-                stride = 2 ** (level - 1)
-                near, far = 1 - y, y
+                total += dot(weight[level, 0], recv[level, 0, j])
+            else:
                 arrived(level, near, j)
-                beyond = lax.rem(me + 2 * stride + (n - 4 * stride) * y, n)
-                send(recv.at[level, near, j], level, far, j, beyond, 1)
-                total = dot(sep_fac[level, near], recv[level, near, j])
+                if level == relay_level:
+                    beyond = lax.rem(me + 2 * stride + (n - 4 * stride) * p, n)
+                    send(recv.at[level, near, j], level, far, j, beyond, 1)
+                total = dot(weight[level, near], recv[level, near, j])
                 arrived(level, far, j)
-                total += dot(sep_fac[level, far], recv[level, far, j])
-            else:
-                arrived(level, 0, j)
-                total = dot(sep_fac[level, 0], recv[level, 0, j])
-                arrived(level, 1, j)
-                total += dot(sep_fac[level, 1], recv[level, 1, j])
-            part = (sep_rhs[level, :, columns].astype(F32) - total).astype(BF16)
-            sol[level, j] = dot(sep_inv[level], part).astype(BF16)
+                total += dot(weight[level, far], recv[level, far, j])
+            sol[level, j] = (free[level, :, columns] - total).astype(BF16)
             if level + 1 < depth:
-                stride = 2**level
+                step = 2**level
+                q = lax.rem(lax.div(me, step), 2)
+                up, down = peer(step), peer(-step)
                 if level + 1 == relay_level:
-                    across = lax.rem(me + stride + (n - 2 * stride) * y, n)
-                    send(sol.at[level, j], level + 1, y, j, across, 0)
+                    send(sol.at[level, j], level + 1, q, j, up + (down - up) * q, 0)
                 else:
-                    send(sol.at[level, j], level + 1, 0, j, peer(stride), 0)
-                    send(sol.at[level, j], level + 1, 1, j, peer(-stride), 1)
+                    send(sol.at[level, j], level + 1, 1 - q, j, down + (up - down) * q, 0)
+                    send(sol.at[level, j], level + 1, q, j, up + (down - up) * q, 1)
             copy = pltpu.make_async_copy(
                 sol.at[level, j], sep_out.at[level, 0, :, pl.ds(j * width, width)], out_sem.at[level, j]
             )
             copy.start()
             out_copies.append(copy)
+        if level + 1 < depth:
+            prepare(level + 1)
+        if level == 0:
+            leaf_level(top)
 
     for copy in sends:
         copy.wait_send()
@@ -204,8 +211,8 @@
     block, loads = leaf_rhs.shape[1:]
     width = loads // CHUNKS
     upper, coupled = leaf_factor.shape[:2]
-    matmuls = leaf_rhs.shape[0] + upper * coupled + 3 * depth
-    hbm = pl.BlockSpec(memory_space=pl.ANY)
+    matmuls = leaf_rhs.shape[0] + upper * coupled + 5 * depth
+    hbm = pl.BlockSpec(memory_space=pltpu.HBM)
     smem = pl.BlockSpec(memory_space=pltpu.SMEM)
     return pl.pallas_call(
         functools.partial(kernel, n, depth, 2 if n == 16 else -1),
@@ -224,6 +231,8 @@
             pltpu.VMEM((depth, 2, block, block), BF16),
             pltpu.VMEM(leaf_rhs.shape, BF16),
             pltpu.VMEM((CHUNKS, block, width), BF16),
+            pltpu.VMEM((depth, 2, block, block), BF16),
+            pltpu.VMEM((depth, block, loads), F32),
             pltpu.VMEM((depth, CHUNKS, block, width), BF16),
             pltpu.VMEM((depth, 2, CHUNKS, block, width), BF16),
             pltpu.SemaphoreType.DMA((3 * LEAF_LEVELS + 2,)),
@@ -233,7 +242,7 @@
             pltpu.SemaphoreType.DMA((depth, 2, CHUNKS)),
         ],
         compiler_params=pltpu.CompilerParams(
-            collective_id=0, has_side_effects=True, vmem_limit_bytes=48 * 2**20
+            collective_id=0, has_side_effects=True, vmem_limit_bytes=64 * 2**20
         ),
         cost_estimate=pl.CostEstimate(
             flops=2 * matmuls * block * block * loads,
@@ -241,7 +250,7 @@
             transcendentals=0,
         ),
         name="tree_solve",
-    )(leaf_rhs, separator_rhs, leaf_inverse, leaf_factor, separator_inverse, separator_factor, block_pattern, link_row)
+    )(leaf_rhs, separator_rhs, leaf_inverse, leaf_factor, separator_inverse, separator_factor, block_pattern.T, link_row)
 
 
 def solution(mesh):

time: 39.6 us -> 36.4 us (0.919)
  the two profiles are of different devices: /device:TPU:1 before, /device:TPU:4 now
where the time goes in v2:
time: 36.4 us; the launch traced here: 36.2 us
  Pallas kernels  31.4 us (86%)
  local copies, waits for them, and re-layouts  3.51 us (10%)
  between operations  1.3 us (4%)
    pallas_call x1, Pallas kernels, shards(): pl.pallas_call(functools.partial(kernel, n, depth, 2 if n == 16 else -1),...  31.4 us
    unnamed x4, local copies, waits for them, and re-layouts  3.51 us

profile of v2, /device:TPU:4, one launch (start us, length us, event | category | flops | bytes accessed | tf_op | source)
XLA Modules:
  0.0 36.2 jit_solution(17766154933079435211)
XLA Ops:
  1.3 31.4 %tree_solve.1 = (bf16[12,256,256]{2,1,0:T(8,128)(2,1)}, bf16[4,1,256,256]{3,2,1,0:T(8,128)(2,1)}) custom-call(bf16[12,256,256]{2,1,0:T(8,128)(2,1)} %rhs_hbm.1, bf16[4,1,256,256]{3,2,1,0:T(8,128)(2,1)} %sep_rhs_hbm.1, bf16[12,256,256]{2,1,0:T(8,128)(2,1)} %inv_hbm.1, bf16[8,4,256,256]{3,2,1,0:T(8,128)(2,1)} %fac_hbm.1, bf16[4,1,256,256]{3,2,1,0:T(8,128)(2,1)} %sep_inv_hbm.1, ...), custom_call_target="tpu_custom_call" | custom-call | flops 2147483648 | bytes 11534336 | tf_op jit(solution)/shard_map/tree_solve/pallas_call | solution.py:217
  32.7 0.0 copy-start
  32.7 2.7 %copy.13 = bf16[12,256,256]{2,1,0:T(8,128)(2,1)} copy(bf16[12,256,256]{2,1,0:T(8,128)(2,1)} %get-tuple-element.4) | data formatting | bytes 3145728
  35.4 0.0 copy-done
  35.4 0.8 %copy.14 = bf16[4,1,256,256]{3,2,1,0:T(8,128)(2,1)} copy(bf16[4,1,256,256]{3,2,1,0:T(8,128)(2,1)S(1)} %copy-done) | data formatting | bytes 1048576
Async XLA Ops:
  32.7 2.7 %copy-start = (bf16[4,1,256,256]{3,2,1,0:T(8,128)(2,1)S(1)}, bf16[4,1,256,256]{3,2,1,0:T(8,128)(2,1)}, u32[]{:S(2)}) copy-start(bf16[4,1,256,256]{3,2,1,0:T(8,128)(2,1)} %get-tuple-element.5) | copy-start | bytes 1572868

commit v3 on v2

--- a/solution.py
+++ b/solution.py
@@ -160,7 +160,8 @@
     loads["sep_fac"].wait()
     loads["sep_rhs"].wait()
     loads["sep_inv"].wait()
-    prepare(0)
+    for level in range(depth):
+        prepare(level)
 
     for level in range(depth):
         stride = 2 ** max(level - 1, 0)
@@ -195,14 +196,27 @@
             )
             copy.start()
             out_copies.append(copy)
-        if level + 1 < depth:
-            prepare(level + 1)
         if level == 0:
             leaf_level(top)
 
     for copy in sends:
         copy.wait_send()
     for copy in out_copies:
+        copy.wait()
+
+
+def place(leaf, sep, leaf_out, sep_out, sem):
+    copies = []
+    for level in range(LEAF_LEVELS):
+        rows = pl.ds(level * LEVEL_ROWS, LEVEL_ROWS)
+        copies.append(pltpu.make_async_copy(leaf.at[rows], leaf_out.at[rows], sem.at[level]))
+    for level in range(sep.shape[0]):
+        copies.append(
+            pltpu.make_async_copy(sep.at[level], sep_out.at[level], sem.at[LEAF_LEVELS + level])
+        )
+    for copy in copies:
+        copy.start()
+    for copy in copies:
         copy.wait()
 
 
@@ -214,8 +228,8 @@
     matmuls = leaf_rhs.shape[0] + upper * coupled + 5 * depth
     hbm = pl.BlockSpec(memory_space=pltpu.HBM)
     smem = pl.BlockSpec(memory_space=pltpu.SMEM)
-    return pl.pallas_call(
-        functools.partial(kernel, n, depth, 2 if n == 16 else -1),
+    solved = pl.pallas_call(
+        functools.partial(kernel, n, depth, -1),
         out_shape=(
             jax.ShapeDtypeStruct(leaf_rhs.shape, BF16),
             jax.ShapeDtypeStruct(separator_rhs.shape, BF16),
@@ -251,6 +265,15 @@
         ),
         name="tree_solve",
     )(leaf_rhs, separator_rhs, leaf_inverse, leaf_factor, separator_inverse, separator_factor, block_pattern.T, link_row)
+    return pl.pallas_call(
+        place,
+        out_shape=tuple(jax.ShapeDtypeStruct(a.shape, a.dtype) for a in solved),
+        in_specs=[hbm] * 2,
+        out_specs=(hbm, hbm),
+        scratch_shapes=[pltpu.SemaphoreType.DMA((LEAF_LEVELS + depth,))],
+        compiler_params=pltpu.CompilerParams(vmem_limit_bytes=64 * 2**20),
+        name="place_results",
+    )(*solved)
 
 
 def solution(mesh):

time: 36.4 us -> 93.3 us (2.56)
  the two profiles are of different devices: /device:TPU:4 before, /device:TPU:1 now
where the time goes in v3:
time: 93.3 us; the launch traced here: 92.7 us
  Pallas kernels  91.5 us (98%)
  between operations  1.29 us (1%)
    pallas_call x1, Pallas kernels, shards(): pl.pallas_call(place, out_shape=tuple((jax.ShapeDtypeStruct(a.shape, a.dt...  64.7 us
    pallas_call x1, Pallas kernels, shards(): pl.pallas_call(functools.partial(kernel, n, depth, -1), out_shape=(jax.Sh...  26.8 us

profile of v3, /device:TPU:1, one launch (start us, length us, event | category | flops | bytes accessed | tf_op | source)
XLA Modules:
  0.0 92.7 jit_solution(4017887252775058511)
XLA Ops:
  1.3 26.8 %tree_solve.1 = (bf16[12,256,256]{2,1,0:T(8,128)(2,1)}, bf16[4,1,256,256]{3,2,1,0:T(8,128)(2,1)}) custom-call(bf16[12,256,256]{2,1,0:T(8,128)(2,1)} %rhs_hbm.1, bf16[4,1,256,256]{3,2,1,0:T(8,128)(2,1)} %sep_rhs_hbm.1, bf16[12,256,256]{2,1,0:T(8,128)(2,1)} %inv_hbm.1, bf16[8,4,256,256]{3,2,1,0:T(8,128)(2,1)} %fac_hbm.1, bf16[4,1,256,256]{3,2,1,0:T(8,128)(2,1)} %sep_inv_hbm.1, ...), custom_call_target="tpu_custom_call" | custom-call | flops 2147483648 | bytes 11534336 | tf_op jit(solution)/shard_map/tree_solve/pallas_call | solution.py:231
  28.0 64.7 %place_results.1 = (bf16[12,256,256]{2,1,0:T(8,128)(2,1)}, bf16[4,1,256,256]{3,2,1,0:T(8,128)(2,1)}) custom-call(bf16[12,256,256]{2,1,0:T(8,128)(2,1)} %get-tuple-element.4.leaf, bf16[4,1,256,256]{3,2,1,0:T(8,128)(2,1)} %get-tuple-element.5.sep), custom_call_target="tpu_custom_call" | custom-call | tf_op jit(solution)/shard_map/place_results/pallas_call | solution.py:268

commit v4 on v3

--- a/solution.py
+++ b/solution.py
@@ -205,18 +205,23 @@
         copy.wait()
 
 
-def place(leaf, sep, leaf_out, sep_out, sem):
-    copies = []
-    for level in range(LEAF_LEVELS):
-        rows = pl.ds(level * LEVEL_ROWS, LEVEL_ROWS)
-        copies.append(pltpu.make_async_copy(leaf.at[rows], leaf_out.at[rows], sem.at[level]))
-    for level in range(sep.shape[0]):
-        copies.append(
-            pltpu.make_async_copy(sep.at[level], sep_out.at[level], sem.at[LEAF_LEVELS + level])
-        )
-    for copy in copies:
+def place(leaf, sep, leaf_out, sep_out, leaf_held, sep_held, in_sem, out_sem):
+    pieces = [
+        (leaf.at[rows], leaf_held.at[rows], leaf_out.at[rows])
+        for rows in (pl.ds(i, 2) for i in range(0, leaf.shape[0], 2))
+    ] + [(sep.at[i], sep_held.at[i], sep_out.at[i]) for i in range(sep.shape[0])]
+    loads = [
+        pltpu.make_async_copy(src, held, in_sem.at[i]) for i, (src, held, _) in enumerate(pieces)
+    ]
+    stores = [
+        pltpu.make_async_copy(held, dst, out_sem.at[i]) for i, (_, held, dst) in enumerate(pieces)
+    ]
+    for copy in loads:
         copy.start()
-    for copy in copies:
+    for copy_in, copy_out in zip(loads, stores):
+        copy_in.wait()
+        copy_out.start()
+    for copy in stores:
         copy.wait()
 
 
@@ -270,7 +275,12 @@
         out_shape=tuple(jax.ShapeDtypeStruct(a.shape, a.dtype) for a in solved),
         in_specs=[hbm] * 2,
         out_specs=(hbm, hbm),
-        scratch_shapes=[pltpu.SemaphoreType.DMA((LEAF_LEVELS + depth,))],
+        scratch_shapes=[
+            pltpu.VMEM(leaf_rhs.shape, BF16),
+            pltpu.VMEM(separator_rhs.shape, BF16),
+            pltpu.SemaphoreType.DMA((leaf_rhs.shape[0] // 2 + depth,)),
+            pltpu.SemaphoreType.DMA((leaf_rhs.shape[0] // 2 + depth,)),
+        ],
         compiler_params=pltpu.CompilerParams(vmem_limit_bytes=64 * 2**20),
         name="place_results",
     )(*solved)

time: 93.3 us -> 31 us (0.33)
  Pallas kernels: 91.5 us -> 29.2 us
    pallas_call x1, Pallas kernels: 64.7 us -> 2.43 us  [shards(): pl.pallas_call(place, out_shape=tuple((jax.ShapeDtypeStruct(a.shape, a.dt...]
where the time goes in v4:
time: 31 us; the launch traced here: 30.5 us
  Pallas kernels  29.2 us (94%)
  between operations  1.29 us (4%)
    pallas_call x1, Pallas kernels, shards(): pl.pallas_call(functools.partial(kernel, n, depth, -1), out_shape=(jax.Sh...  26.8 us
    pallas_call x1, Pallas kernels, shards(): pl.pallas_call(place, out_shape=tuple((jax.ShapeDtypeStruct(a.shape, a.dt...  2.43 us

profile of v4, /device:TPU:1, one launch (start us, length us, event | category | flops | bytes accessed | tf_op | source)
XLA Modules:
  0.0 30.5 jit_solution(15363129054910079025)
XLA Ops:
  1.3 26.8 %tree_solve.1 = (bf16[12,256,256]{2,1,0:T(8,128)(2,1)}, bf16[4,1,256,256]{3,2,1,0:T(8,128)(2,1)}) custom-call(bf16[12,256,256]{2,1,0:T(8,128)(2,1)} %rhs_hbm.1, bf16[4,1,256,256]{3,2,1,0:T(8,128)(2,1)} %sep_rhs_hbm.1, bf16[12,256,256]{2,1,0:T(8,128)(2,1)} %inv_hbm.1, bf16[8,4,256,256]{3,2,1,0:T(8,128)(2,1)} %fac_hbm.1, bf16[4,1,256,256]{3,2,1,0:T(8,128)(2,1)} %sep_inv_hbm.1, ...), custom_call_target="tpu_custom_call" | custom-call | flops 2147483648 | bytes 11534336 | tf_op jit(solution)/shard_map/tree_solve/pallas_call | solution.py:236
  28.0 2.4 %place_results.1 = (bf16[12,256,256]{2,1,0:T(8,128)(2,1)}, bf16[4,1,256,256]{3,2,1,0:T(8,128)(2,1)}) custom-call(bf16[12,256,256]{2,1,0:T(8,128)(2,1)} %get-tuple-element.4.leaf, bf16[4,1,256,256]{3,2,1,0:T(8,128)(2,1)} %get-tuple-element.5.sep), custom_call_target="tpu_custom_call" | custom-call | tf_op jit(solution)/shard_map/place_results/pallas_call | solution.py:273

commit v5 on v4

--- a/solution.py
+++ b/solution.py
@@ -9,7 +9,8 @@
 
 LEVEL_ROWS = 4
 LEAF_LEVELS = 3
-CHUNKS = 2
+CHUNKS = 4
+PAIR = 2
 F32 = jnp.float32
 BF16 = jnp.bfloat16
 
@@ -43,6 +44,7 @@
     weight,
     free,
     sol,
+    turned,
     recv,
     load_sem,
     leaf_sem,
@@ -52,7 +54,7 @@
 ):
     me = lax.axis_index("rows")
     coupled = fac.shape[1]
-    width = sol.shape[-1]
+    width = sol.shape[1] // CHUNKS
 
     def peer(by):
         return lax.rem(me + (by % n), n)
@@ -118,18 +120,20 @@
     for name in ("fac", "rhs", "inv"):
         loads[(name, top)].wait()
     link_row = link[0]
-    edge_block = dot(inv[link_row], residual(link_row, jnp.maximum(link_row - LEVEL_ROWS, 0))).astype(BF16)
-    for j in range(CHUNKS):
-        edge[j] = edge_block[:, j * width : (j + 1) * width]
+    edge_block = dot(inv[link_row], residual(link_row, jnp.maximum(link_row - LEVEL_ROWS, 0)))
+    edge[...] = edge_block.T.astype(BF16)
 
     pl.semaphore_wait(barrier, len(offsets))
+
+    def chunk(j):
+        return pl.ds(j * width, width)
 
     sends = []
 
     def send(src, level, side, j, to, slot):
         copy = pltpu.make_async_remote_copy(
             src_ref=src,
-            dst_ref=recv.at[level, side, j],
+            dst_ref=recv.at[level, side, chunk(j)],
             send_sem=send_sem.at[level, slot, j],
             recv_sem=recv_sem.at[level, side, j],
             device_id={"rows": to},
@@ -140,8 +144,8 @@
 
     def arrived(level, side, j):
         pltpu.make_async_remote_copy(
-            src_ref=edge.at[j],
-            dst_ref=recv.at[level, side, j],
+            src_ref=edge.at[chunk(j)],
+            dst_ref=recv.at[level, side, chunk(j)],
             send_sem=send_sem.at[level, 0, j],
             recv_sem=recv_sem.at[level, side, j],
             device_id={"rows": peer(1)},
@@ -149,55 +153,68 @@
         ).wait_recv()
 
     for j in range(CHUNKS):
-        send(edge.at[j], 0, 0, j, peer(1), 0)
+        send(edge.at[chunk(j)], 0, 0, j, peer(1), 0)
 
     def prepare(level):
         node_inv = sep_inv[level]
         for side in range(2):
-            weight[level, side] = dot(node_inv, sep_fac[level, side]).astype(BF16)
-        free[level] = dot(node_inv, sep_rhs[level])
+            weight[level, side] = dot(node_inv, sep_fac[level, side]).T.astype(BF16)
+        free[level] = dot(node_inv, sep_rhs[level]).T
 
     loads["sep_fac"].wait()
     loads["sep_rhs"].wait()
     loads["sep_inv"].wait()
-    for level in range(depth):
+    for level in range(2):
         prepare(level)
+
+    def sep_write(level, pair):
+        lanes = PAIR * width
+        turned[level, pair] = sol[level, pl.ds(pair * lanes, lanes)].astype(F32).T.astype(BF16)
+        copy = pltpu.make_async_copy(
+            turned.at[level, pair],
+            sep_out.at[level, 0, :, pl.ds(pair * lanes, lanes)],
+            out_sem.at[level, pair],
+        )
+        copy.start()
+        out_copies.append(copy)
 
     for level in range(depth):
         stride = 2 ** max(level - 1, 0)
         p = lax.rem(lax.div(me, stride), 2)
         near, far = 1 - p, p
         for j in range(CHUNKS):
-            columns = slice(j * width, (j + 1) * width)
+            here = chunk(j)
             if level == 0:
-                total = dot(weight[level, 1], edge[j])
+                total = dot(edge[here], weight[level, 1])
                 arrived(level, 0, j)
-                total += dot(weight[level, 0], recv[level, 0, j])
+                total += dot(recv[level, 0, here], weight[level, 0])
             else:
                 arrived(level, near, j)
                 if level == relay_level:
                     beyond = lax.rem(me + 2 * stride + (n - 4 * stride) * p, n)
-                    send(recv.at[level, near, j], level, far, j, beyond, 1)
-                total = dot(weight[level, near], recv[level, near, j])
+                    send(recv.at[level, near, here], level, far, j, beyond, 1)
+                total = dot(recv[level, near, here], weight[level, near])
                 arrived(level, far, j)
-                total += dot(weight[level, far], recv[level, far, j])
-            sol[level, j] = (free[level, :, columns] - total).astype(BF16)
+                total += dot(recv[level, far, here], weight[level, far])
+            sol[level, here] = (free[level, here] - total).astype(BF16)
             if level + 1 < depth:
                 step = 2**level
                 q = lax.rem(lax.div(me, step), 2)
                 up, down = peer(step), peer(-step)
                 if level + 1 == relay_level:
-                    send(sol.at[level, j], level + 1, q, j, up + (down - up) * q, 0)
+                    send(sol.at[level, here], level + 1, q, j, up + (down - up) * q, 0)
                 else:
-                    send(sol.at[level, j], level + 1, 1 - q, j, down + (up - down) * q, 0)
-                    send(sol.at[level, j], level + 1, q, j, up + (down - up) * q, 1)
-            copy = pltpu.make_async_copy(
-                sol.at[level, j], sep_out.at[level, 0, :, pl.ds(j * width, width)], out_sem.at[level, j]
-            )
-            copy.start()
-            out_copies.append(copy)
+                    send(sol.at[level, here], level + 1, 1 - q, j, down + (up - down) * q, 0)
+                    send(sol.at[level, here], level + 1, q, j, up + (down - up) * q, 1)
+            if level + 1 == depth and j % PAIR == PAIR - 1:
+                sep_write(level, j // PAIR)
         if level == 0:
             leaf_level(top)
+            for later in range(2, depth):
+                prepare(later)
+        if level + 1 < depth:
+            for pair in range(CHUNKS // PAIR):
+                sep_write(level, pair)
 
     for copy in sends:
         copy.wait_send()
@@ -249,14 +266,15 @@
             pltpu.VMEM((depth, block, block), BF16),
             pltpu.VMEM((depth, 2, block, block), BF16),
             pltpu.VMEM(leaf_rhs.shape, BF16),
-            pltpu.VMEM((CHUNKS, block, width), BF16),
+            pltpu.VMEM((loads, block), BF16),
             pltpu.VMEM((depth, 2, block, block), BF16),
-            pltpu.VMEM((depth, block, loads), F32),
-            pltpu.VMEM((depth, CHUNKS, block, width), BF16),
-            pltpu.VMEM((depth, 2, CHUNKS, block, width), BF16),
+            pltpu.VMEM((depth, loads, block), F32),
+            pltpu.VMEM((depth, loads, block), BF16),
+            pltpu.VMEM((depth, CHUNKS // PAIR, block, PAIR * width), BF16),
+            pltpu.VMEM((depth, 2, loads, block), BF16),
             pltpu.SemaphoreType.DMA((3 * LEAF_LEVELS + 2,)),
             pltpu.SemaphoreType.DMA((LEAF_LEVELS,)),
-            pltpu.SemaphoreType.DMA((depth, CHUNKS)),
+            pltpu.SemaphoreType.DMA((depth, CHUNKS // PAIR)),
             pltpu.SemaphoreType.DMA((depth, 2, CHUNKS)),
             pltpu.SemaphoreType.DMA((depth, 2, CHUNKS)),
         ],

time: 31 us -> 32.2 us (1.039)
  Pallas kernels: 29.2 us -> 30.4 us
    pallas_call x1, Pallas kernels: 26.8 us -> 28 us  [shards(): pl.pallas_call(functools.partial(kernel, n, depth, -1), out_shape=(jax.Sh...]
where the time goes in v5:
time: 32.2 us; the launch traced here: 31.7 us
  Pallas kernels  30.4 us (94%)
  between operations  1.29 us (4%)
    pallas_call x1, Pallas kernels, shards(): pl.pallas_call(functools.partial(kernel, n, depth, -1), out_shape=(jax.Sh...  28 us
    pallas_call x1, Pallas kernels, shards(): pl.pallas_call(place, out_shape=tuple((jax.ShapeDtypeStruct(a.shape, a.dt...  2.43 us

profile of v5, /device:TPU:1, one launch (start us, length us, event | category | flops | bytes accessed | tf_op | source)
XLA Modules:
  0.0 31.7 jit_solution(126874058522172008)
XLA Ops:
  1.3 28.0 %tree_solve.1 = (bf16[12,256,256]{2,1,0:T(8,128)(2,1)}, bf16[4,1,256,256]{3,2,1,0:T(8,128)(2,1)}) custom-call(bf16[12,256,256]{2,1,0:T(8,128)(2,1)} %rhs_hbm.1, bf16[4,1,256,256]{3,2,1,0:T(8,128)(2,1)} %sep_rhs_hbm.1, bf16[12,256,256]{2,1,0:T(8,128)(2,1)} %inv_hbm.1, bf16[8,4,256,256]{3,2,1,0:T(8,128)(2,1)} %fac_hbm.1, bf16[4,1,256,256]{3,2,1,0:T(8,128)(2,1)} %sep_inv_hbm.1, ...), custom_call_target="tpu_custom_call" | custom-call | flops 2147483648 | bytes 11534336 | tf_op jit(solution)/shard_map/tree_solve/pallas_call | solution.py:253
  29.3 2.4 %place_results.1 = (bf16[12,256,256]{2,1,0:T(8,128)(2,1)}, bf16[4,1,256,256]{3,2,1,0:T(8,128)(2,1)}) custom-call(bf16[12,256,256]{2,1,0:T(8,128)(2,1)} %get-tuple-element.4.leaf, bf16[4,1,256,256]{3,2,1,0:T(8,128)(2,1)} %get-tuple-element.5.sep), custom_call_target="tpu_custom_call" | custom-call | tf_op jit(solution)/shard_map/place_results/pallas_call | solution.py:291

commit v6 on v4

--- a/solution.py
+++ b/solution.py
@@ -44,11 +44,14 @@
     free,
     sol,
     recv,
+    weight_above,
+    sent_rest,
     load_sem,
     leaf_sem,
     out_sem,
     send_sem,
     recv_sem,
+    above_sem,
 ):
     me = lax.axis_index("rows")
     coupled = fac.shape[1]
@@ -63,6 +66,15 @@
         copy = pltpu.make_async_copy(src, dst, load_sem.at[len(loads)])
         copy.start()
         loads[name] = copy
+
+    def load_nodes(name, levels):
+        load(("sep_inv", name), sep_inv_hbm.at[levels, 0], sep_inv.at[levels])
+        load(("sep_fac", name), sep_fac_hbm.at[levels, 0], sep_fac.at[levels])
+        load(("sep_rhs", name), sep_rhs_hbm.at[levels, 0], sep_rhs.at[levels])
+
+    def wait_nodes(name):
+        for what in ("sep_inv", "sep_fac", "sep_rhs"):
+            loads[(what, name)].wait()
 
     for level in range(LEAF_LEVELS):
         rows = pl.ds(level * LEVEL_ROWS, LEVEL_ROWS)
@@ -71,9 +83,9 @@
             load(("fac", level), fac_hbm.at[low], fac.at[low])
         load(("rhs", level), rhs_hbm.at[rows], rhs.at[rows])
         load(("inv", level), inv_hbm.at[rows], inv.at[rows])
-    load("sep_fac", sep_fac_hbm.at[:, 0], sep_fac)
-    load("sep_rhs", sep_rhs_hbm.at[:, 0], sep_rhs)
-    load("sep_inv", sep_inv_hbm.at[:, 0], sep_inv)
+        if level == 0:
+            load_nodes("first", pl.ds(0, 1))
+    load_nodes("rest", pl.ds(1, depth - 1))
 
     offsets = sorted({(sign * 2**h) % n for h in range(depth - 1) for sign in (1, -1)})
     barrier = pltpu.get_barrier_semaphore()
@@ -113,6 +125,26 @@
         for name in ("fac", "rhs", "inv"):
             loads[(name, level)].wait()
         leaf_level(level)
+
+    def prepare(level):
+        node_inv = sep_inv[level]
+        for side in range(2):
+            weight[level, side] = dot(node_inv, sep_fac[level, side]).astype(BF16)
+        free[level] = dot(node_inv, sep_rhs[level])
+
+    wait_nodes("first")
+    prepare(0)
+
+    pl.semaphore_wait(barrier, len(offsets))
+    weight_copy = pltpu.make_async_remote_copy(
+        src_ref=weight.at[0, 0],
+        dst_ref=weight_above,
+        send_sem=above_sem.at[0],
+        recv_sem=above_sem.at[1],
+        device_id={"rows": peer(-1)},
+        device_id_type=pl.DeviceIdType.MESH,
+    )
+    weight_copy.start()
 
     top = LEAF_LEVELS - 1
     for name in ("fac", "rhs", "inv"):
@@ -121,8 +153,6 @@
     edge_block = dot(inv[link_row], residual(link_row, jnp.maximum(link_row - LEVEL_ROWS, 0))).astype(BF16)
     for j in range(CHUNKS):
         edge[j] = edge_block[:, j * width : (j + 1) * width]
-
-    pl.semaphore_wait(barrier, len(offsets))
 
     sends = []
 
@@ -150,18 +180,11 @@
 
     for j in range(CHUNKS):
         send(edge.at[j], 0, 0, j, peer(1), 0)
-
-    def prepare(level):
-        node_inv = sep_inv[level]
-        for side in range(2):
-            weight[level, side] = dot(node_inv, sep_fac[level, side]).astype(BF16)
-        free[level] = dot(node_inv, sep_rhs[level])
-
-    loads["sep_fac"].wait()
-    loads["sep_rhs"].wait()
-    loads["sep_inv"].wait()
-    for level in range(depth):
-        prepare(level)
+        columns = slice(j * width, (j + 1) * width)
+        rest = free[0, :, columns] - dot(weight[0, 1], edge[j])
+        free[0, :, columns] = rest
+        sent_rest[j] = rest.astype(BF16)
+        send(sent_rest.at[j], 1, 1, j, peer(-1), 1)
 
     for level in range(depth):
         stride = 2 ** max(level - 1, 0)
@@ -170,7 +193,12 @@
         for j in range(CHUNKS):
             columns = slice(j * width, (j + 1) * width)
             if level == 0:
-                total = dot(weight[level, 1], edge[j])
+                arrived(level, 0, j)
+                total = dot(weight[level, 0], recv[level, 0, j])
+            elif level == 1:
+                arrived(level, 1, j)
+                above = recv[level, 1, j].astype(F32) - dot(weight_above[...], edge[j])
+                total = dot(weight[level, 1], above.astype(BF16))
                 arrived(level, 0, j)
                 total += dot(weight[level, 0], recv[level, 0, j])
             else:
@@ -186,7 +214,9 @@
                 step = 2**level
                 q = lax.rem(lax.div(me, step), 2)
                 up, down = peer(step), peer(-step)
-                if level + 1 == relay_level:
+                if level == 0:
+                    send(sol.at[level, j], 1, 0, j, up, 0)
+                elif level + 1 == relay_level:
                     send(sol.at[level, j], level + 1, q, j, up + (down - up) * q, 0)
                 else:
                     send(sol.at[level, j], level + 1, 1 - q, j, down + (up - down) * q, 0)
@@ -197,6 +227,12 @@
             copy.start()
             out_copies.append(copy)
         if level == 0:
+            wait_nodes("rest")
+        if level + 1 < depth:
+            prepare(level + 1)
+        if level == 0:
+            weight_copy.wait()
+        if level == 1:
             leaf_level(top)
 
     for copy in sends:
@@ -254,11 +290,14 @@
             pltpu.VMEM((depth, block, loads), F32),
             pltpu.VMEM((depth, CHUNKS, block, width), BF16),
             pltpu.VMEM((depth, 2, CHUNKS, block, width), BF16),
-            pltpu.SemaphoreType.DMA((3 * LEAF_LEVELS + 2,)),
+            pltpu.VMEM((block, block), BF16),
+            pltpu.VMEM((CHUNKS, block, width), BF16),
+            pltpu.SemaphoreType.DMA((3 * LEAF_LEVELS + 5,)),
             pltpu.SemaphoreType.DMA((LEAF_LEVELS,)),
             pltpu.SemaphoreType.DMA((depth, CHUNKS)),
             pltpu.SemaphoreType.DMA((depth, 2, CHUNKS)),
             pltpu.SemaphoreType.DMA((depth, 2, CHUNKS)),
+            pltpu.SemaphoreType.DMA((2,)),
         ],
         compiler_params=pltpu.CompilerParams(
             collective_id=0, has_side_effects=True, vmem_limit_bytes=64 * 2**20

time: 31 us -> 32.6 us (1.052)
  the two profiles are of different devices: /device:TPU:1 before, /device:TPU:0 now
where the time goes in v6:
time: 32.6 us; the launch traced here: 32.5 us
  Pallas kernels  31.2 us (96%)
  between operations  1.29 us (4%)
    pallas_call x1, Pallas kernels, shards(): pl.pallas_call(functools.partial(kernel, n, depth, -1), out_shape=(jax.Sh...  28.8 us
    pallas_call x1, Pallas kernels, shards(): pl.pallas_call(place, out_shape=tuple((jax.ShapeDtypeStruct(a.shape, a.dt...  2.43 us

profile of v6, /device:TPU:0, one launch (start us, length us, event | category | flops | bytes accessed | tf_op | source)
XLA Modules:
  0.0 32.5 jit_solution(9866904731532819989)
XLA Ops:
  1.3 28.8 %tree_solve.1 = (bf16[12,256,256]{2,1,0:T(8,128)(2,1)}, bf16[4,1,256,256]{3,2,1,0:T(8,128)(2,1)}) custom-call(bf16[12,256,256]{2,1,0:T(8,128)(2,1)} %rhs_hbm.1, bf16[4,1,256,256]{3,2,1,0:T(8,128)(2,1)} %sep_rhs_hbm.1, bf16[12,256,256]{2,1,0:T(8,128)(2,1)} %inv_hbm.1, bf16[8,4,256,256]{3,2,1,0:T(8,128)(2,1)} %fac_hbm.1, bf16[4,1,256,256]{3,2,1,0:T(8,128)(2,1)} %sep_inv_hbm.1, ...), custom_call_target="tpu_custom_call" | custom-call | flops 2147483648 | bytes 11534336 | tf_op jit(solution)/shard_map/tree_solve/pallas_call | solution.py:272
  30.0 2.4 %place_results.1 = (bf16[12,256,256]{2,1,0:T(8,128)(2,1)}, bf16[4,1,256,256]{3,2,1,0:T(8,128)(2,1)}) custom-call(bf16[12,256,256]{2,1,0:T(8,128)(2,1)} %get-tuple-element.4.leaf, bf16[4,1,256,256]{3,2,1,0:T(8,128)(2,1)} %get-tuple-element.5.sep), custom_call_target="tpu_custom_call" | custom-call | tf_op jit(solution)/shard_map/place_results/pallas_call | solution.py:312

commit v7 on v6

--- a/solution.py
+++ b/solution.py
@@ -44,14 +44,11 @@
     free,
     sol,
     recv,
-    weight_above,
-    sent_rest,
     load_sem,
     leaf_sem,
     out_sem,
     send_sem,
     recv_sem,
-    above_sem,
 ):
     me = lax.axis_index("rows")
     coupled = fac.shape[1]
@@ -135,17 +132,6 @@
     wait_nodes("first")
     prepare(0)
 
-    pl.semaphore_wait(barrier, len(offsets))
-    weight_copy = pltpu.make_async_remote_copy(
-        src_ref=weight.at[0, 0],
-        dst_ref=weight_above,
-        send_sem=above_sem.at[0],
-        recv_sem=above_sem.at[1],
-        device_id={"rows": peer(-1)},
-        device_id_type=pl.DeviceIdType.MESH,
-    )
-    weight_copy.start()
-
     top = LEAF_LEVELS - 1
     for name in ("fac", "rhs", "inv"):
         loads[(name, top)].wait()
@@ -153,6 +139,8 @@
     edge_block = dot(inv[link_row], residual(link_row, jnp.maximum(link_row - LEVEL_ROWS, 0))).astype(BF16)
     for j in range(CHUNKS):
         edge[j] = edge_block[:, j * width : (j + 1) * width]
+
+    pl.semaphore_wait(barrier, len(offsets))
 
     sends = []
 
@@ -180,11 +168,6 @@
 
     for j in range(CHUNKS):
         send(edge.at[j], 0, 0, j, peer(1), 0)
-        columns = slice(j * width, (j + 1) * width)
-        rest = free[0, :, columns] - dot(weight[0, 1], edge[j])
-        free[0, :, columns] = rest
-        sent_rest[j] = rest.astype(BF16)
-        send(sent_rest.at[j], 1, 1, j, peer(-1), 1)
 
     for level in range(depth):
         stride = 2 ** max(level - 1, 0)
@@ -193,12 +176,7 @@
         for j in range(CHUNKS):
             columns = slice(j * width, (j + 1) * width)
             if level == 0:
-                arrived(level, 0, j)
-                total = dot(weight[level, 0], recv[level, 0, j])
-            elif level == 1:
-                arrived(level, 1, j)
-                above = recv[level, 1, j].astype(F32) - dot(weight_above[...], edge[j])
-                total = dot(weight[level, 1], above.astype(BF16))
+                total = dot(weight[level, 1], edge[j])
                 arrived(level, 0, j)
                 total += dot(weight[level, 0], recv[level, 0, j])
             else:
@@ -214,9 +192,7 @@
                 step = 2**level
                 q = lax.rem(lax.div(me, step), 2)
                 up, down = peer(step), peer(-step)
-                if level == 0:
-                    send(sol.at[level, j], 1, 0, j, up, 0)
-                elif level + 1 == relay_level:
+                if level + 1 == relay_level:
                     send(sol.at[level, j], level + 1, q, j, up + (down - up) * q, 0)
                 else:
                     send(sol.at[level, j], level + 1, 1 - q, j, down + (up - down) * q, 0)
@@ -230,8 +206,6 @@
             wait_nodes("rest")
         if level + 1 < depth:
             prepare(level + 1)
-        if level == 0:
-            weight_copy.wait()
         if level == 1:
             leaf_level(top)
 
@@ -290,14 +264,11 @@
             pltpu.VMEM((depth, block, loads), F32),
             pltpu.VMEM((depth, CHUNKS, block, width), BF16),
             pltpu.VMEM((depth, 2, CHUNKS, block, width), BF16),
-            pltpu.VMEM((block, block), BF16),
-            pltpu.VMEM((CHUNKS, block, width), BF16),
             pltpu.SemaphoreType.DMA((3 * LEAF_LEVELS + 5,)),
             pltpu.SemaphoreType.DMA((LEAF_LEVELS,)),
             pltpu.SemaphoreType.DMA((depth, CHUNKS)),
             pltpu.SemaphoreType.DMA((depth, 2, CHUNKS)),
             pltpu.SemaphoreType.DMA((depth, 2, CHUNKS)),
-            pltpu.SemaphoreType.DMA((2,)),
         ],
         compiler_params=pltpu.CompilerParams(
             collective_id=0, has_side_effects=True, vmem_limit_bytes=64 * 2**20

time: 32.6 us -> 31 us (0.951)
  the two profiles are of different devices: /device:TPU:0 before, /device:TPU:1 now
where the time goes in v7:
time: 31 us; the launch traced here: 30.6 us
  Pallas kernels  29.3 us (95%)
  between operations  1.29 us (4%)
    pallas_call x1, Pallas kernels, shards(): pl.pallas_call(functools.partial(kernel, n, depth, -1), out_shape=(jax.Sh...  26.9 us
    pallas_call x1, Pallas kernels, shards(): pl.pallas_call(place, out_shape=tuple((jax.ShapeDtypeStruct(a.shape, a.dt...  2.43 us

profile of v7, /device:TPU:1, one launch (start us, length us, event | category | flops | bytes accessed | tf_op | source)
XLA Modules:
  0.0 30.6 jit_solution(6667855973766369203)
XLA Ops:
  1.3 26.9 %tree_solve.1 = (bf16[12,256,256]{2,1,0:T(8,128)(2,1)}, bf16[4,1,256,256]{3,2,1,0:T(8,128)(2,1)}) custom-call(bf16[12,256,256]{2,1,0:T(8,128)(2,1)} %rhs_hbm.1, bf16[4,1,256,256]{3,2,1,0:T(8,128)(2,1)} %sep_rhs_hbm.1, bf16[12,256,256]{2,1,0:T(8,128)(2,1)} %inv_hbm.1, bf16[8,4,256,256]{3,2,1,0:T(8,128)(2,1)} %fac_hbm.1, bf16[4,1,256,256]{3,2,1,0:T(8,128)(2,1)} %sep_inv_hbm.1, ...), custom_call_target="tpu_custom_call" | custom-call | flops 2147483648 | bytes 11534336 | tf_op jit(solution)/shard_map/tree_solve/pallas_call | solution.py:246
  28.2 2.4 %place_results.1 = (bf16[12,256,256]{2,1,0:T(8,128)(2,1)}, bf16[4,1,256,256]{3,2,1,0:T(8,128)(2,1)}) custom-call(bf16[12,256,256]{2,1,0:T(8,128)(2,1)} %get-tuple-element.4.leaf, bf16[4,1,256,256]{3,2,1,0:T(8,128)(2,1)} %get-tuple-element.5.sep), custom_call_target="tpu_custom_call" | custom-call | tf_op jit(solution)/shard_map/place_results/pallas_call | solution.py:283
